TPU v7x, 128 devices: a whole 4x4x4 slice. The times are simulated.
128 devices in a mesh: pipe: 8 (over y, core), expert: 16 (over x, z).
Axes of the slice: x: 4, y: 4, z: 4, core: 2. Of those that a mesh axis runs over, the one named last changes fastest.
Arguments:
- upstream_first: bfloat16 [8, 2048, 7168], P('pipe', 'expert'), may hold values from -6 to 6
- upstream_last: bfloat16 [2048, 7168], P('expert'), may hold values from -6 to 6
- saved_input: bfloat16 [8, 2, 2048, 7168], P('pipe', None, 'expert'), may hold values from -64 to 64
- norm_gain: float32 [8, 7168], P('pipe'), may hold values from 0.5 to 1.5
- router_weight: float32 [8, 7168, 4], P('pipe'), may hold values from -0.0625 to 0.0625
- routes: int32 [8, 2, 2048, 2], P('pipe', None, 'expert'), may hold values from 0 to 3, all different within a row; in each aligned block of 128 rows (0 to 127, 128 to 255, ..., all dimensions but the last counted through in order) at most 72 rows name the same one
- w_gate: bfloat16 [8, 16, 1792, 1024], P('pipe', 'expert'), may hold values from -0.0625 to 0.0625
- w_up: bfloat16 [8, 16, 1792, 1024], P('pipe', 'expert'), may hold values from -0.0625 to 0.0625
- w_down: bfloat16 [8, 16, 1024, 1792], P('pipe', 'expert'), may hold values from -0.1875 to 0.1875
- saved_preact: bfloat16 [8, 2, 16, 288, 2048], P('pipe', None, 'expert'), may hold values from -6 to 6
Outputs:
- grad_first: bfloat16 [8, 2048, 7168], P('pipe', 'expert')
- grad_second: bfloat16 [8, 2048, 7168], P('pipe', 'expert')
Inputs may be any that keep to these rules, and one draw needn't show every extreme that they name: `routes`: each row names 2 different experts. Within the rows of one device of one section and wave, no expert is named by more than 72 rows, a bound that some block reaches.
All inputs are finite; a program needn't handle non-finite values.
Results may differ from a plain program's by a relative error of at most 0.011.
Values may be sent and summed in bfloat16 or wider, within the bound.
No kernel may reach another device: no remote copies, remote signals or barrier semaphores. Data moves between devices by JAX's collectives and lax.ppermute only.
A program may use at most 128 MiB of HBM per device.

v0:
```python
import jax
import jax.numpy as jnp
from jax import lax
from jax.sharding import PartitionSpec as P

CAP = 72


epsilon = 1e-06
route_scale = 2.5


def swapped(value, axis, apart):
    return lax.ppermute(value, axis, [(i, i ^ 1 << apart) for i in range(lax.axis_size(axis))])


def passed_along(value, axis, steps):
    count = lax.axis_size(axis)
    first, last = (max(0, -steps), min(count, count - steps))
    return lax.ppermute(value, axis, [(source, source + steps) for source in range(first, last)])


def activation_step(hidden_grad, acts, hidden):
    gate_pre = acts[:, :hidden].astype(jnp.float32)
    up_pre = acts[:, hidden:].astype(jnp.float32)
    sigmoid_g = jax.nn.sigmoid(gate_pre)
    silu_g = gate_pre * sigmoid_g
    score_grad = jnp.sum(hidden_grad * silu_g * up_pre, axis=-1).astype(jnp.bfloat16)
    gate_grad = (hidden_grad * up_pre * sigmoid_g * (1.0 + gate_pre * (1.0 - sigmoid_g))).astype(
        jnp.bfloat16
    )
    up_grad = (hidden_grad * silu_g).astype(jnp.bfloat16)
    return (score_grad, jnp.concatenate([gate_grad, up_grad], axis=1))


def section(upstream, saved_rows, gain, router, routing, gate_rows, up_rows, down_cols, acts):
    tok_rows, model_width = upstream.shape
    experts = router.shape[1]
    top_count = routing.shape[1]
    hidden = down_cols.shape[0]
    groups = lax.axis_size("expert")
    split_count = groups // experts
    part_width = model_width // split_count
    capacity = CAP
    share = acts.shape[0]
    member = lax.axis_index("expert") % split_count
    levels = split_count.bit_length() - 1
    inputs = saved_rows.astype(jnp.float32)
    inverse = lax.rsqrt(jnp.mean(inputs * inputs, axis=-1, keepdims=True) + epsilon)
    normed = inputs * inverse * gain
    logits = jnp.dot(
        normed, router, precision=lax.Precision.HIGHEST, preferred_element_type=jnp.float32
    )
    affinity = jax.nn.sigmoid(logits)
    chosen = jnp.take_along_axis(affinity, routing, axis=1)
    total_sum = jnp.sum(chosen, axis=-1, keepdims=True)
    weights = route_scale * chosen / total_sum
    expert_flat = routing.reshape(-1)
    onehot = (expert_flat[:, None] == jnp.arange(experts, dtype=jnp.int32)).astype(jnp.int32)
    ranking = jnp.sum(onehot * (jnp.cumsum(onehot, axis=0) - 1), axis=-1)
    token_index = jnp.arange(tok_rows * top_count, dtype=jnp.int32) // top_count
    slot_rows = (
        (expert_flat[:, None] * split_count + jnp.arange(split_count, dtype=jnp.int32)[None, :])
        * capacity
        + ranking[:, None]
    ).reshape(-1)
    pieces = upstream.reshape(tok_rows, split_count, part_width)[token_index].reshape(
        -1, part_width
    )
    outgoing = jnp.zeros((groups * capacity, part_width), jnp.bfloat16).at[slot_rows].set(pieces)
    arrived = lax.all_to_all(
        outgoing.reshape(groups, capacity, part_width),
        "expert",
        split_axis=0,
        concat_axis=0,
        tiled=True,
    )
    arrived = arrived.reshape(groups * capacity, part_width)
    partial_value = lax.dot_general(
        arrived, down_cols, (((1,), (1,)), ((), ())), preferred_element_type=jnp.float32
    ).astype(jnp.bfloat16)
    current = partial_value
    for level_num in range(levels):
        bit_pos = levels - 1 - level_num
        halves = current.reshape(2, -1, current.shape[-1])
        upper_half = member // 2**bit_pos % 2 == 1
        kept_half = jnp.where(upper_half, halves[1], halves[0])
        sending = jnp.where(upper_half, halves[0], halves[1])
        if level_num == 0:
            received = swapped(sending, "expert", bit_pos)
        else:
            received = swapped(sending, "expert", bit_pos)
        current = kept_half.astype(jnp.float32) + received.astype(jnp.float32)
    score_grad, gathered = activation_step(current, acts, hidden)
    for bit_pos in range(levels):
        received = swapped(gathered, "expert", bit_pos)
        upper_half = member // 2**bit_pos % 2 == 1
        gathered = jnp.where(
            upper_half,
            jnp.concatenate([received, gathered], axis=0),
            jnp.concatenate([gathered, received], axis=0),
        )
    scores_all = lax.dynamic_update_slice_in_dim(
        jnp.zeros((groups * capacity,), jnp.bfloat16), score_grad, member * share, 0
    )
    back_rows = lax.dot_general(
        gathered[:, :hidden],
        gate_rows,
        (((1,), (1,)), ((), ())),
        preferred_element_type=jnp.float32,
    )
    back_rows = back_rows + lax.dot_general(
        gathered[:, hidden:], up_rows, (((1,), (1,)), ((), ())), preferred_element_type=jnp.float32
    )
    back_rows = back_rows.astype(jnp.bfloat16)
    returned, score_back = (
        lax.all_to_all(
            back_rows.reshape(groups, capacity, part_width),
            "expert",
            split_axis=0,
            concat_axis=0,
            tiled=True,
        ),
        lax.all_to_all(
            scores_all.reshape(groups, capacity), "expert", split_axis=0, concat_axis=0, tiled=True
        ),
    )
    picked = (
        returned.reshape(groups * capacity, part_width)[slot_rows]
        .reshape(tok_rows, top_count, model_width)
        .astype(jnp.float32)
    )
    score_rows = score_back.reshape(experts, split_count, capacity)[expert_flat, :, ranking]
    score_pick = jnp.sum(score_rows.astype(jnp.float32), axis=-1).reshape(tok_rows, top_count)
    normed_grad = jnp.sum(weights[:, :, None] * picked, axis=1)
    mixed = jnp.sum(score_pick * chosen, axis=-1, keepdims=True) / total_sum
    chosen_grad = route_scale * (score_pick - mixed) / total_sum
    logit_pair = chosen_grad * chosen * (1.0 - chosen)
    columns = (routing[:, :, None] == jnp.arange(experts, dtype=jnp.int32)).astype(jnp.float32)
    dense_grad = jnp.sum(logit_pair[:, :, None] * columns, axis=1)
    normed_grad = normed_grad + jnp.dot(
        dense_grad, router.T, precision=lax.Precision.HIGHEST, preferred_element_type=jnp.float32
    )
    gained = normed_grad * gain
    input_grad = inverse * gained - inputs * inverse**3 * jnp.mean(
        inputs * gained, axis=-1, keepdims=True
    )
    return (upstream.astype(jnp.float32) + input_grad).astype(jnp.bfloat16)


def on_device(
    upstream_first,
    upstream_last,
    saved_input,
    norm_gain,
    router_weight,
    routes,
    w_gate,
    w_up,
    w_down,
    saved_preact,
):
    first_grad = section(
        upstream_first[0],
        saved_input[0, 0],
        norm_gain[0],
        router_weight[0],
        routes[0, 0],
        w_gate[0, 0],
        w_up[0, 0],
        w_down[0, 0],
        saved_preact[0, 0, 0],
    )
    shifted = passed_along(first_grad, "pipe", -1)
    is_last = lax.axis_index("pipe") == lax.axis_size("pipe") - 1
    upstream = jnp.where(is_last, upstream_last, shifted)
    second = section(
        upstream,
        saved_input[0, 1],
        norm_gain[0],
        router_weight[0],
        routes[0, 1],
        w_gate[0, 0],
        w_up[0, 0],
        w_down[0, 0],
        saved_preact[0, 1, 0],
    )
    return (first_grad[None], second[None])


def solution(mesh):
    return jax.shard_map(
        on_device,
        mesh=mesh,
        in_specs=(
            P("pipe", "expert", None),
            P("expert", None),
            P("pipe", None, "expert", None),
            P("pipe", None),
            P("pipe", None, None),
            P("pipe", None, "expert", None),
            P("pipe", "expert", None, None),
            P("pipe", "expert", None, None),
            P("pipe", "expert", None, None),
            P("pipe", None, "expert", None, None),
        ),
        out_specs=(P("pipe", "expert", None), P("pipe", "expert", None)),
        check_vma=False,
    )
```

profile of v0, /device:TPU:8, one launch (start us, length us, event | category | flops | bytes accessed | tf_op | source)
XLA Modules:
  0.0 736.3 jit_solution(7874853660084471038)
XLA Ops:
  4.3 3.6 reshape_squeeze.2
  7.9 5.3 gather_fusion
  13.2 6.8 reshape.539
  20.0 9.4 %scatter_custom_fusion = bf16[1152,1792]{1,0:T(8,128)(2,1)} fusion(s32[1024]{0:T(1024)S(1)} %bitcast.200, bf16[1024,1792]{1,0:T(8,128)(2,1)} %reshape.539, bf16[]{:T(256)} %constant.144.clone.1), kind=kCustom, calls=%fused_computation.70 | custom fusion | bytes 4129280 | tf_op jit(solution)/shard_map/scatter | solution.py:70
  29.4 8.1 %all-to-all-start = ((bf16[16,72,1792]{2,1,0:T(8,128)(2,1)}), bf16[16,72,1792]{2,1,0:T(8,128)(2,1)}, u32[]{:S(2)}, u32[]{:S(2)}) async-start(bf16[16,72,1792]{2,1,0:T(8,128)(2,1)} %bitcast.188), calls=%async_computation | async-start | bytes 8257536 | tf_op jit(solution)/shard_map/all_to_all | solution.py:71
  37.6 60.7 %all-to-all-done = bf16[16,72,1792]{2,1,0:T(8,128)(2,1)} async-done(((bf16[16,72,1792]{2,1,0:T(8,128)(2,1)}), bf16[16,72,1792]{2,1,0:T(8,128)(2,1)}, u32[]{:S(2)}, u32[]{:S(2)}) %all-to-all-start) | async-done | bytes 4128800 | tf_op jit(solution)/shard_map/all_to_all | solution.py:71
  98.3 7.8 %convolution_convert_fusion.1 = bf16[1152,1024]{1,0:T(8,128)(2,1)S(1)} fusion(bf16[1152,1792]{1,0:T(8,128)(2,1)} %bitcast.12, bf16[1,1,1024,1792]{3,2,1,0:T(8,128)(2,1)} %param.20), kind=kOutput, calls=%fused_computation.33 | convolution fusion | flops 4229038080 | bytes 10158080 | tf_op jit(solution)/shard_map/dot_general | solution.py:79
  107.2 27.7 %collective-permute-done = bf16[576,1024]{1,0:T(8,128)(2,1)} collective-permute-done((bf16[576,1024]{1,0:T(8,128)(2,1)}, bf16[576,1024]{1,0:T(8,128)(2,1)}, u32[]{:S(2)}, u32[]{:S(2)}) %collective-permute-start) | collective-permute-done | bytes 1179680 | tf_op jit(solution)/shard_map/ppermute | solution.py:14
  137.4 24.7 %collective-permute-done.1 = f32[288,1024]{1,0:T(8,128)S(1)} collective-permute-done((f32[288,1024]{1,0:T(8,128)S(1)}, f32[288,1024]{1,0:T(8,128)S(1)}, u32[]{:S(2)}, u32[]{:S(2)}) %collective-permute-start.1) | collective-permute-done | bytes 1179680 | tf_op jit(solution)/shard_map/ppermute | solution.py:14
  163.8 23.7 %collective-permute-done.2 = bf16[288,2048]{1,0:T(8,128)(2,1)S(1)} collective-permute-done((bf16[288,2048]{1,0:T(8,128)(2,1)S(1)}, bf16[288,2048]{1,0:T(8,128)(2,1)S(1)}, u32[]{:S(2)}, u32[]{:S(2)}) %collective-permute-start.2) | collective-permute-done | bytes 1179680 | tf_op jit(solution)/shard_map/ppermute | solution.py:14
  187.5 10.0 %maximum_select_fusion.2 = bf16[576,2048]{1,0:T(8,128)(2,1)} fusion(bf16[288,1024]{1,0:T(8,128)(2,1)S(1)} %get-tuple-element.20, bf16[288,1024]{1,0:T(8,128)(2,1)S(1)} %get-tuple-element.19, bf16[288,2048]{1,0:T(8,128)(2,1)S(1)} %collective-permute-done.2, pred[]{:T(512)S(6)} %eq.91), kind=kLoop, calls=%fused_computation.64 | loop fusion | flops 15335424 | bytes 4718593 | tf_op jit(solution)/shard_map/jit(_where)/select_n | solution.py:98
  199.3 12.5 %all-to-all-start.2 = ((bf16[16,1,72]{2,1,0:T(2,128)(2,1)}), bf16[16,1,72]{2,1,0:T(2,128)(2,1)S(1)}, u32[]{:S(2)}, u32[]{:S(2)}) async-start(bf16[16,1,72]{2,1,0:T(2,128)(2,1)} %all_to_all.32), calls=%async_computation.2 | async-start | bytes 16384 | tf_op jit(solution)/shard_map/all_to_all | solution.py:124
  211.7 36.1 %collective-permute-done.3 = bf16[576,2048]{1,0:T(8,128)(2,1)} collective-permute-done((bf16[576,2048]{1,0:T(8,128)(2,1)}, bf16[576,2048]{1,0:T(8,128)(2,1)}, u32[]{:S(2)}, u32[]{:S(2)}) %collective-permute-start.3) | collective-permute-done | bytes 2359328 | tf_op jit(solution)/shard_map/ppermute | solution.py:14
  247.8 5.0 maximum_select_fusion
  252.9 4.5 fusion.32
  257.4 6.1 fusion.2
  263.5 13.1 %all-to-all-start.1 = ((bf16[16,72,1792]{2,1,0:T(8,128)(2,1)}), bf16[16,72,1792]{2,1,0:T(8,128)(2,1)}, u32[]{:S(2)}, u32[]{:S(2)}) async-start(bf16[16,72,1792]{2,1,0:T(8,128)(2,1)} %bitcast.190), calls=%async_computation.1 | async-start | bytes 8257536 | tf_op jit(solution)/shard_map/all_to_all | solution.py:117
  279.0 4.6 fusion.92
  283.6 2.4 gather_fusion.6
  288.6 35.1 %all-to-all-done.1 = bf16[16,72,1792]{2,1,0:T(8,128)(2,1)} async-done(((bf16[16,72,1792]{2,1,0:T(8,128)(2,1)}), bf16[16,72,1792]{2,1,0:T(8,128)(2,1)}, u32[]{:S(2)}, u32[]{:S(2)}) %all-to-all-start.1) | async-done | bytes 4128800 | tf_op jit(solution)/shard_map/all_to_all | solution.py:117
  323.7 10.7 %gather_fusion.1 = bf16[1024,1792]{1,0:T(8,128)(2,1)} fusion(bf16[1152,1792]{1,0:T(8,128)(2,1)} %bitcast.18, s32[1024]{0:T(1024)S(1)} %broadcast_clamp_fusion.1), kind=kCustom, calls=%fused_computation.3 | custom fusion | bytes 7344128 | tf_op jit(solution)/shard_map/gather | solution.py:129
  334.3 9.3 %reshape.476 = f32[128,2,7168]{2,1,0:T(2,128)} reshape(bf16[1024,1792]{1,0:T(8,128)(2,1)} %gather_fusion.1) | data formatting | bytes 11010048 | tf_op jit(solution)/shard_map/convert_element_type | solution.py:131
  343.6 11.4 %multiply_reduce_fusion.1 = f32[128,7168]{1,0:T(8,128)S(1)} fusion(f32[128,2,7168]{2,1,0:T(2,128)} %reshape.476, f32[128,2]{1,0:T(8,128)S(1)} %copy.56), kind=kLoop, calls=%fused_computation.19 | loop fusion | flops 2752512 | bytes 11011072 | tf_op jit(solution)/shard_map/reduce_sum | solution.py:135
  355.0 4.2 fusion.20
  364.8 18.4 %collective-permute-done.4 = bf16[128,7168]{1,0:T(8,128)(2,1)} collective-permute-done((bf16[128,7168]{1,0:T(8,128)(2,1)S(1)}, bf16[128,7168]{1,0:T(8,128)(2,1)}, u32[]{:S(2)}, u32[]{:S(2)}) %collective-permute-start.4) | collective-permute-done | bytes 1835040 | tf_op jit(solution)/shard_map/ppermute | solution.py:20
  387.2 6.8 gather_fusion.3
  394.0 6.8 reshape.547
  400.9 9.4 %scatter_custom_fusion.1 = bf16[1152,1792]{1,0:T(8,128)(2,1)} fusion(s32[1024]{0:T(1024)S(1)} %bitcast.202, bf16[1024,1792]{1,0:T(8,128)(2,1)} %reshape.547, bf16[]{:T(256)} %constant.144.clone.1), kind=kCustom, calls=%fused_computation.68 | custom fusion | bytes 4129280 | tf_op jit(solution)/shard_map/scatter | solution.py:70
  410.2 59.5 %all_to_all.40 = bf16[16,72,1792]{2,1,0:T(8,128)(2,1)S(1)} all-to-all(bf16[16,72,1792]{2,1,0:T(8,128)(2,1)} %bitcast.189), channel_id=1, replica_groups=mesh['pipe'=8,'expert'=16] {'expert'}, dimensions={0} | all-to-all | bytes 8257536 | tf_op jit(solution)/shard_map/all_to_all | solution.py:71
  469.8 4.8 convolution_convert_fusion
  476.9 28.1 %collective-permute-done.5 = bf16[576,1024]{1,0:T(8,128)(2,1)S(1)} collective-permute-done((bf16[576,1024]{1,0:T(8,128)(2,1)S(1)}, bf16[576,1024]{1,0:T(8,128)(2,1)S(1)}, u32[]{:S(2)}, u32[]{:S(2)}) %collective-permute-start.5) | collective-permute-done | bytes 1179680 | tf_op jit(solution)/shard_map/ppermute | solution.py:14
  506.4 27.5 %collective-permute-done.6 = f32[288,1024]{1,0:T(8,128)S(1)} collective-permute-done((f32[288,1024]{1,0:T(8,128)S(1)}, f32[288,1024]{1,0:T(8,128)S(1)}, u32[]{:S(2)}, u32[]{:S(2)}) %collective-permute-start.6) | collective-permute-done | bytes 1179680 | tf_op jit(solution)/shard_map/ppermute | solution.py:14
  535.9 26.6 %collective-permute-done.7 = bf16[288,2048]{1,0:T(8,128)(2,1)S(1)} collective-permute-done((bf16[288,2048]{1,0:T(8,128)(2,1)S(1)}, bf16[288,2048]{1,0:T(8,128)(2,1)S(1)}, u32[]{:S(2)}, u32[]{:S(2)}) %collective-permute-start.7) | collective-permute-done | bytes 1179680 | tf_op jit(solution)/shard_map/ppermute | solution.py:14
  562.5 10.0 %maximum_select_fusion.3 = bf16[576,2048]{1,0:T(8,128)(2,1)} fusion(bf16[288,1024]{1,0:T(8,128)(2,1)S(1)} %get-tuple-element.16, bf16[288,1024]{1,0:T(8,128)(2,1)S(1)} %get-tuple-element.15, bf16[288,2048]{1,0:T(8,128)(2,1)S(1)} %collective-permute-done.7, pred[]{:T(512)S(6)} %eq.91), kind=kLoop, calls=%fused_computation.65 | loop fusion | flops 15335424 | bytes 4718593 | tf_op jit(solution)/shard_map/jit(_where)/select_n | solution.py:98
  574.2 5.1 all-to-all-start.5
  579.3 46.6 %collective-permute-done.8 = bf16[576,2048]{1,0:T(8,128)(2,1)} collective-permute-done((bf16[576,2048]{1,0:T(8,128)(2,1)}, bf16[576,2048]{1,0:T(8,128)(2,1)}, u32[]{:S(2)}, u32[]{:S(2)}) %collective-permute-start.8) | collective-permute-done | bytes 2359328 | tf_op jit(solution)/shard_map/ppermute | solution.py:14
  625.9 5.0 maximum_select_fusion.1
  631.0 4.5 fusion.30
  635.5 6.1 fusion.3
  641.6 4.7 all-to-all-start.4
  646.8 4.7 fusion.80
  651.4 2.4 gather_fusion.7
  656.4 42.0 %all-to-all-done.4 = bf16[16,72,1792]{2,1,0:T(8,128)(2,1)} async-done(((bf16[16,72,1792]{2,1,0:T(8,128)(2,1)}), bf16[16,72,1792]{2,1,0:T(8,128)(2,1)}, u32[]{:S(2)}, u32[]{:S(2)}) %all-to-all-start.4) | async-done | bytes 4128800 | tf_op jit(solution)/shard_map/all_to_all | solution.py:117
  698.3 10.7 %gather_fusion.4 = bf16[1024,1792]{1,0:T(8,128)(2,1)} fusion(bf16[1152,1792]{1,0:T(8,128)(2,1)} %bitcast.33, s32[1024]{0:T(1024)S(1)} %broadcast_clamp_fusion), kind=kCustom, calls=%fused_computation.6 | custom fusion | bytes 7344128 | tf_op jit(solution)/shard_map/gather | solution.py:129
  709.0 9.3 %reshape.478 = f32[128,2,7168]{2,1,0:T(2,128)} reshape(bf16[1024,1792]{1,0:T(8,128)(2,1)} %gather_fusion.4) | data formatting | bytes 11010048 | tf_op jit(solution)/shard_map/convert_element_type | solution.py:131
  718.3 11.2 %multiply_reduce_fusion = f32[128,7168]{1,0:T(8,128)S(1)} fusion(f32[128,2,7168]{2,1,0:T(2,128)} %reshape.478, f32[128,2]{1,0:T(8,128)S(1)} %copy.68), kind=kLoop, calls=%fused_computation.18 | loop fusion | flops 2752512 | bytes 11011072 | tf_op jit(solution)/shard_map/reduce_sum | solution.py:135
  729.5 3.8 fusion.25
  733.4 2.5 fusion.46
  (138 shorter events, 35.3 us)
Async XLA Ops:
  0.6 278.3 %copy-start = (f32[1,7168,4]{1,2,0:T(4,128)S(1)}, f32[1,7168,4]{1,2,0:T(4,128)}, u32[]{:S(2)}) copy-start(f32[1,7168,4]{1,2,0:T(4,128)} %param.16) | copy-start | bytes 344068
  29.4 68.9 %all-to-all-start = ((bf16[16,72,1792]{2,1,0:T(8,128)(2,1)}), bf16[16,72,1792]{2,1,0:T(8,128)(2,1)}, u32[]{:S(2)}, u32[]{:S(2)}) async-start(bf16[16,72,1792]{2,1,0:T(8,128)(2,1)} %bitcast.188), calls=%async_computation | async-start | bytes 8257536 | tf_op jit(solution)/shard_map/all_to_all | solution.py:71
  107.2 27.7 %collective-permute-start = (bf16[576,1024]{1,0:T(8,128)(2,1)}, bf16[576,1024]{1,0:T(8,128)(2,1)}, u32[]{:S(2)}, u32[]{:S(2)}) collective-permute-start(bf16[576,1024]{1,0:T(8,128)(2,1)} %broadcast_select_fusion.2), channel_id=1, source_target_pairs={{0,2},{1,3},{2,0},{3,1},{4,6},{5,7},{6,4},{7,5},{8,10},{9,11},{10,... | collective-permute-start | bytes 3538952 | tf_op jit(solution)/shard_map/ppermute | solution.py:14
  107.2 30.0 %copy-start.4 = (bf16[1,2,1,288,2048]{4,3,2,1,0:T(8,128)(2,1)S(1)}, bf16[1,2,1,288,2048]{4,3,2,1,0:T(8,128)(2,1)}, u32[]{:S(2)}) copy-start(bf16[1,2,1,288,2048]{4,3,2,1,0:T(8,128)(2,1)} %param.21) | copy-start | bytes 7077892
  137.1 25.0 %collective-permute-start.1 = (f32[288,1024]{1,0:T(8,128)S(1)}, f32[288,1024]{1,0:T(8,128)S(1)}, u32[]{:S(2)}, u32[]{:S(2)}) collective-permute-start(f32[288,1024]{1,0:T(8,128)S(1)} %slice_select_fusion.1), channel_id=1, source_target_pairs={{0,1},{1,0},{2,3},{3,2},{4,5},{5,4},{6,7},{7,6},{8,9},{9,8},{10,11... | collective-permute-start | bytes 3538952 | tf_op jit(solution)/shard_map/ppermute | solution.py:14
  163.4 24.1 %collective-permute-start.2 = (bf16[288,2048]{1,0:T(8,128)(2,1)S(1)}, bf16[288,2048]{1,0:T(8,128)(2,1)S(1)}, u32[]{:S(2)}, u32[]{:S(2)}) collective-permute-start(bf16[288,2048]{1,0:T(8,128)(2,1)S(1)} %pad_maximum_fusion), channel_id=1, source_target_pairs={{0,1},{1,0},{2,3},{3,2},{4,5},{5,4},{6,7},{7,6},{8,9},{9,8},{10,11... | collective-permute-start | bytes 3538952 | tf_op jit(solution)/shard_map/ppermute | solution.py:14
  197.5 50.3 %collective-permute-start.3 = (bf16[576,2048]{1,0:T(8,128)(2,1)}, bf16[576,2048]{1,0:T(8,128)(2,1)}, u32[]{:S(2)}, u32[]{:S(2)}) collective-permute-start(bf16[576,2048]{1,0:T(8,128)(2,1)} %maximum_select_fusion.2), channel_id=1, source_target_pairs={{0,2},{1,3},{2,0},{3,1},{4,6},{5,7},{6,4},{7,5},{8,10},{9,11},{10,... | collective-permute-start | bytes 7077896 | tf_op jit(solution)/shard_map/ppermute | solution.py:14
  199.3 64.2 %all-to-all-start.2 = ((bf16[16,1,72]{2,1,0:T(2,128)(2,1)}), bf16[16,1,72]{2,1,0:T(2,128)(2,1)S(1)}, u32[]{:S(2)}, u32[]{:S(2)}) async-start(bf16[16,1,72]{2,1,0:T(2,128)(2,1)} %all_to_all.32), calls=%async_computation.2 | async-start | bytes 16384 | tf_op jit(solution)/shard_map/all_to_all | solution.py:124
  211.7 41.1 %copy-start.10 = (bf16[1,1,1792,1024]{3,2,1,0:T(8,128)(2,1)S(1)}, bf16[1,1,1792,1024]{3,2,1,0:T(8,128)(2,1)}, u32[]{:S(2)}) copy-start(bf16[1,1,1792,1024]{3,2,1,0:T(8,128)(2,1)} %param.19) | copy-start | bytes 11010052
  252.9 4.5 copy-start.12
  263.5 13.3 %copy-start.7 = (s32[1,2,128,2]{2,3,1,0:T(2,128)S(1)}, s32[1,2,128,2]{2,3,1,0:T(2,128)}, u32[]{:S(2)}) copy-start(s32[1,2,128,2]{2,3,1,0:T(2,128)} %param.17) | copy-start | bytes 6148
  263.5 15.5 %copy-start.6 = (f32[1,7168]{1,0:T(1,128)S(1)}, f32[1,7168]{1,0:T(1,128)}, u32[]{:S(2)}) copy-start(f32[1,7168]{1,0:T(1,128)} %param.15) | copy-start | bytes 86020
  263.5 60.2 %all-to-all-start.1 = ((bf16[16,72,1792]{2,1,0:T(8,128)(2,1)}), bf16[16,72,1792]{2,1,0:T(8,128)(2,1)}, u32[]{:S(2)}, u32[]{:S(2)}) async-start(bf16[16,72,1792]{2,1,0:T(8,128)(2,1)} %bitcast.190), calls=%async_computation.1 | async-start | bytes 8257536 | tf_op jit(solution)/shard_map/all_to_all | solution.py:117
  343.6 11.4 %copy-start.1 = (bf16[1,2,128,7168]{3,2,1,0:T(8,128)(2,1)S(1)}, bf16[1,2,128,7168]{3,2,1,0:T(8,128)(2,1)}, u32[]{:S(2)}) copy-start(bf16[1,2,128,7168]{3,2,1,0:T(8,128)(2,1)} %param.14) | copy-start | bytes 11010052
  355.0 4.2 copy-start.3
  360.5 4.3 copy-start.5
  360.5 22.7 %collective-permute-start.4 = (bf16[128,7168]{1,0:T(8,128)(2,1)S(1)}, bf16[128,7168]{1,0:T(8,128)(2,1)}, u32[]{:S(2)}, u32[]{:S(2)}) collective-permute-start(bf16[128,7168]{1,0:T(8,128)(2,1)S(1)} %fusion.14), channel_id=1, source_target_pairs={{16,0},{32,16},{48,32},{64,48},{80,64},{96,80},{112,96},{17,1},{33... | collective-permute-start | bytes 5505032 | tf_op jit(solution)/shard_map/ppermute | solution.py:20
  410.2 59.5 %copy-start.9 = (bf16[1,1,1024,1792]{3,2,1,0:T(8,128)(2,1)S(1)}, bf16[1,1,1024,1792]{3,2,1,0:T(8,128)(2,1)}, u32[]{:S(2)}) copy-start(bf16[1,1,1024,1792]{3,2,1,0:T(8,128)(2,1)} %param.20) | copy-start | bytes 11010052
  474.7 30.3 %collective-permute-start.5 = (bf16[576,1024]{1,0:T(8,128)(2,1)S(1)}, bf16[576,1024]{1,0:T(8,128)(2,1)S(1)}, u32[]{:S(2)}, u32[]{:S(2)}) collective-permute-start(bf16[576,1024]{1,0:T(8,128)(2,1)S(1)} %broadcast_select_fusion.1), channel_id=1, source_target_pairs={{0,2},{1,3},{2,0},{3,1},{4,6},{5,7},{6,4},{7,5},{8,10},{9,11},{10,... | collective-permute-start | bytes 3538952 | tf_op jit(solution)/shard_map/ppermute | solution.py:14
  505.9 28.1 %collective-permute-start.6 = (f32[288,1024]{1,0:T(8,128)S(1)}, f32[288,1024]{1,0:T(8,128)S(1)}, u32[]{:S(2)}, u32[]{:S(2)}) collective-permute-start(f32[288,1024]{1,0:T(8,128)S(1)} %slice_select_fusion), channel_id=1, source_target_pairs={{0,1},{1,0},{2,3},{3,2},{4,5},{5,4},{6,7},{7,6},{8,9},{9,8},{10,11... | collective-permute-start | bytes 3538952 | tf_op jit(solution)/shard_map/ppermute | solution.py:14
  535.3 27.2 %collective-permute-start.7 = (bf16[288,2048]{1,0:T(8,128)(2,1)S(1)}, bf16[288,2048]{1,0:T(8,128)(2,1)S(1)}, u32[]{:S(2)}, u32[]{:S(2)}) collective-permute-start(bf16[288,2048]{1,0:T(8,128)(2,1)S(1)} %pad_maximum_fusion.1), channel_id=1, source_target_pairs={{0,1},{1,0},{2,3},{3,2},{4,5},{5,4},{6,7},{7,6},{8,9},{9,8},{10,11... | collective-permute-start | bytes 3538952 | tf_op jit(solution)/shard_map/ppermute | solution.py:14
  572.5 53.4 %collective-permute-start.8 = (bf16[576,2048]{1,0:T(8,128)(2,1)}, bf16[576,2048]{1,0:T(8,128)(2,1)}, u32[]{:S(2)}, u32[]{:S(2)}) collective-permute-start(bf16[576,2048]{1,0:T(8,128)(2,1)} %maximum_select_fusion.3), channel_id=1, source_target_pairs={{0,2},{1,3},{2,0},{3,1},{4,6},{5,7},{6,4},{7,5},{8,10},{9,11},{10,... | collective-permute-start | bytes 7077896 | tf_op jit(solution)/shard_map/ppermute | solution.py:14
  574.2 67.4 %all-to-all-start.5 = ((bf16[16,1,72]{2,1,0:T(2,128)(2,1)}), bf16[16,1,72]{2,1,0:T(2,128)(2,1)S(1)}, u32[]{:S(2)}, u32[]{:S(2)}) async-start(bf16[16,1,72]{2,1,0:T(2,128)(2,1)} %all_to_all.33), calls=%async_computation.5 | async-start | bytes 16384 | tf_op jit(solution)/shard_map/all_to_all | solution.py:124
  579.3 51.7 %copy-start.11 = (bf16[1,1,1792,1024]{3,2,1,0:T(8,128)(2,1)S(1)}, bf16[1,1,1792,1024]{3,2,1,0:T(8,128)(2,1)}, u32[]{:S(2)}) copy-start(bf16[1,1,1792,1024]{3,2,1,0:T(8,128)(2,1)} %param.19) | copy-start | bytes 11010052
  631.0 4.5 copy-start.13
  641.6 56.8 %all-to-all-start.4 = ((bf16[16,72,1792]{2,1,0:T(8,128)(2,1)}), bf16[16,72,1792]{2,1,0:T(8,128)(2,1)}, u32[]{:S(2)}, u32[]{:S(2)}) async-start(bf16[16,72,1792]{2,1,0:T(8,128)(2,1)} %bitcast.191), calls=%async_computation.4 | async-start | bytes 8257536 | tf_op jit(solution)/shard_map/all_to_all | solution.py:117
  651.4 5.0 copy-start.8
  718.3 11.2 %copy-start.2 = (bf16[1,2,128,7168]{3,2,1,0:T(8,128)(2,1)S(1)}, bf16[1,2,128,7168]{3,2,1,0:T(8,128)(2,1)}, u32[]{:S(2)}) copy-start(bf16[1,2,128,7168]{3,2,1,0:T(8,128)(2,1)} %param.14) | copy-start | bytes 11010052
where the time goes:
time: 745 us; the launch traced here: 736 us
  waiting for transfers between devices  397 us (53%)
  local copies, waits for them, and re-layouts  106 us (14%)
  other arithmetic  70.5 us (9%)
  blocking collectives  59.5 us (8%)
  matrix products  51 us (7%)
  starting transfers between devices  50.9 us (7%)
    ppermute x8, waiting for transfers between devices, swapped(): lax.ppermute(value, axis, [(i, i ^ 1 << apart) for i in range(lax.axis_si...  241 us
    all_to_all x2, waiting for transfers between devices, section(): lax.all_to_all(back_rows.reshape(groups, capacity, part_width), 'expert',...  77 us
    all_to_all x1, waiting for transfers between devices, section(): lax.all_to_all(outgoing.reshape(groups, capacity, part_width), 'expert',...  60.7 us
    all_to_all x1, blocking collectives, section(): lax.all_to_all(outgoing.reshape(groups, capacity, part_width), 'expert',...  59.5 us
    select_n x4, other arithmetic, section(): jnp.where(upper_half, jnp.concatenate([received, gathered], axis=0), jnp....  30.1 us
    reduce_sum x2, other arithmetic, section(): normed_grad = jnp.sum(weights[:, :, None] * picked, axis=1)  22.6 us
    gather x2, local copies, waits for them, and re-layouts, section(): returned.reshape(groups * capacity, part_width)[slot_rows]  21.3 us
    scatter x2, local copies, waits for them, and re-layouts, section(): jnp.zeros((groups * capacity, part_width), jnp.bfloat16).at[slot_rows]  18.7 us
  transfers between devices with their start and end apart: 14, of which 12 were waited for; matrix products, arithmetic and copies ran while one was open for 8% of the time, Pallas kernels for 0%

commit v1 on v0

v1 whole, which is shorter than its diff:
```python
import jax
import jax.numpy as jnp
from jax import lax
from jax.sharding import Mesh
from jax.sharding import PartitionSpec as P

CAP = 72
EXPERTS = 4
CHUNKS = ((0, 1), (2, 3))

epsilon = 1e-06
route_scale = 2.5


def turned(value, axis, offset):
    if offset == 0:
        return value
    count = lax.axis_size(axis)
    return lax.ppermute(value, axis, [(i, (i + offset) % count) for i in range(count)])


def pick(stacked, index):
    return lax.dynamic_index_in_dim(stacked, index, 0, keepdims=False)


def split_in_two(value):
    high = value.astype(jnp.bfloat16)
    return high, (value - high.astype(jnp.float32)).astype(jnp.bfloat16)


def token_values(saved_input, gain, router, routes):
    waves, tokens, width = saved_input.shape
    flat = saved_input.reshape(waves * tokens, width)
    inputs = flat.astype(jnp.float32)
    inverse = lax.rsqrt(jnp.mean(inputs * inputs, axis=-1) + epsilon)
    scaled = gain[:, None] * router
    high = scaled.astype(jnp.bfloat16)
    rest = scaled - high.astype(jnp.float32)
    middle = rest.astype(jnp.bfloat16)
    low = (rest - middle.astype(jnp.float32)).astype(jnp.bfloat16)
    parts = jnp.dot(
        flat, jnp.concatenate([high, middle, low], axis=1), preferred_element_type=jnp.float32
    ).reshape(waves * tokens, 3, EXPERTS)
    logits = (parts[:, 0] + (parts[:, 1] + parts[:, 2])) * inverse[:, None]
    affinity = jax.nn.sigmoid(logits).reshape(waves, tokens, EXPERTS)
    routed = (routes[..., None] == jnp.arange(EXPERTS, dtype=jnp.int32)).astype(jnp.float32)
    chosen = jnp.sum(routed * affinity[:, :, None, :], axis=-1)
    total = jnp.sum(chosen, axis=-1, keepdims=True)
    weights = route_scale * chosen / total
    own = (1.0 - chosen) * (1.0 - chosen / total)
    other = -(chosen * (1.0 - chosen) / total)[:, :, ::-1]
    spread = own[..., None] * routed + other[..., None] * routed[:, :, ::-1]
    names = routes.reshape(waves, -1)
    count = names.shape[1]
    places = jnp.arange(count, dtype=jnp.int32)
    earlier = (names[:, :, None] == names[:, None, :]) & (places[None, :] < places[:, None])
    rank = jnp.sum(earlier.astype(jnp.int32), axis=-1)
    slots = (names * CAP + rank).reshape(waves, tokens, 2).astype(jnp.float32)
    packed = jnp.concatenate(
        [
            slots,
            weights,
            inverse.reshape(waves, tokens, 1),
            spread.reshape(waves, tokens, 2 * EXPERTS),
            jnp.zeros((waves, tokens, 3), jnp.float32),
        ],
        axis=-1,
    )
    return inverse.reshape(waves, tokens), jnp.swapaxes(packed, 1, 2)


def on_device(
    upstream_first,
    upstream_last,
    saved_input,
    norm_gain,
    router_weight,
    routes,
    w_gate,
    w_up,
    w_down,
    saved_preact,
):
    side = lax.axis_size("z")
    x_at, z_at = lax.axis_index("x"), lax.axis_index("z")
    pipe_count = lax.axis_size("pipe")
    is_last = lax.axis_index("pipe") == pipe_count - 1
    upstream_first, saved_input = upstream_first[0], saved_input[0]
    gain, router, routes = norm_gain[0], router_weight[0], routes[0]
    down_cols, preact = w_down[0, 0], saved_preact[0, :, 0]
    tokens, width = upstream_first.shape
    part = width // side
    hidden = down_cols.shape[0]

    def feature_block(value, index):
        return lax.dynamic_slice_in_dim(value, index % side * part, part, value.ndim - 1)

    def by_source(blocks):
        stacked = jnp.stack(blocks)
        return [pick(stacked, (z_at - source) % side) for source in range(side)]

    def spread_features(value):
        return by_source(
            [turned(feature_block(value, z_at + off), "z", off) for off in range(side)]
        )

    def gather_features(blocks):
        stacked = jnp.stack(blocks)
        got = jnp.stack(
            [turned(pick(stacked, (z_at + off) % side), "z", off) for off in range(side)]
        )
        return jnp.concatenate([pick(got, (z_at - q) % side) for q in range(side)], axis=1)

    def pipe_back(value):
        return lax.ppermute(value, "pipe", [(i, i - 1) for i in range(1, pipe_count)])

    first_blocks = spread_features(upstream_first)
    inverse, packed = token_values(saved_input, gain, router, routes)
    facts = jnp.stack(by_source([turned(packed, "z", off) for off in range(side)]))
    input_blocks = spread_features(saved_input[0])
    last_blocks = []
    for off in range(side):
        value = feature_block(upstream_last, z_at + off)
        if off:
            stage = pipe_count - 1
            value = lax.ppermute(
                value,
                ("pipe", "z"),
                [(stage * side + i, stage * side + (i + off) % side) for i in range(side)],
            )
        last_blocks.append(value)
    last_blocks = by_source(last_blocks)

    gain_block = feature_block(gain, z_at)
    router_block = lax.dynamic_slice_in_dim(router, z_at * part, part, 0)
    router_high, router_low = split_in_two(router_block)
    back_weight = jnp.concatenate(
        [
            w_gate[0, 0],
            w_up[0, 0],
            router_high,
            router_high,
            router_low,
            jnp.zeros((part, 128 - 3 * EXPERTS), jnp.bfloat16),
        ],
        axis=1,
    )

    rows = jnp.arange(CAP, dtype=jnp.int32)[:, None]

    def matches(wave, source, expert, k):
        place = facts[source, wave, k].astype(jnp.int32) - expert * CAP
        return place[None, :] == rows

    def placing(wave, source, off):
        expert = (x_at + off) % side
        both = matches(wave, source, expert, 0) | matches(wave, source, expert, 1)
        return both.astype(jnp.bfloat16)

    def weighing(wave, source, off):
        expert = (x_at - off) % side
        value = sum(
            jnp.where(matches(wave, source, expert, k), facts[source, wave, 2 + k][None, :], 0.0)
            for k in range(2)
        )
        return value.astype(jnp.bfloat16)

    def slot_spread(off):
        expert = (x_at + off) % side
        value = 0.0
        for k in range(2):
            match = jnp.stack(
                [
                    jnp.stack([matches(wave, source, expert, k) for source in range(side)])
                    for wave in range(2)
                ]
            ).astype(jnp.float32)
            fact = jnp.swapaxes(facts[:, :, 5 + 4 * k : 9 + 4 * k], 0, 1)
            value = value + jnp.einsum("wsrt,wsat->wsra", match, fact, precision="highest")
        return turned(value.reshape(2, side * CAP, EXPERTS), "x", off)

    spreads = pick(jnp.stack([slot_spread(off) for off in range(side)]), (x_at - z_at) % side)

    def experts_of(wave, sources, blocks):
        depth = len(sources) * CAP
        upstream = jnp.stack(blocks)
        arrived = {}
        for off in (2, 1, 3, 0):
            place = jnp.stack([placing(wave, source, off) for source in sources])
            sent = jnp.einsum(
                "srt,stf->srf", place, upstream, preferred_element_type=jnp.bfloat16
            ).reshape(depth, part)
            arrived[off] = turned(sent, "x", off)
        arrived = jnp.concatenate([arrived[off] for off in range(side)])
        partial = lax.dot_general(
            arrived, down_cols, (((1,), (1,)), ((), ())), preferred_element_type=jnp.float32
        ).astype(jnp.bfloat16).reshape(side, depth, hidden)
        pieces = [pick(partial, (x_at - z_at - off) % side) for off in range(side)]
        half = hidden // 2
        upward = turned(pieces[2][:, :half], "z", 1)
        downward = turned(pieces[2][:, half:], "z", -1)
        f32 = jnp.float32
        up_sum = jnp.concatenate(
            [(pieces[1][:, :half].astype(f32) + upward.astype(f32)).astype(jnp.bfloat16), pieces[1][:, half:]],
            axis=1,
        )
        down_sum = jnp.concatenate(
            [pieces[3][:, :half], (pieces[3][:, half:].astype(f32) + downward.astype(f32)).astype(jnp.bfloat16)],
            axis=1,
        )
        hidden_grad = (
            pieces[0].astype(f32)
            + turned(up_sum, "z", 1).astype(f32)
            + turned(down_sum, "z", -1).astype(f32)
        )
        start = sources[0] * CAP
        acts = preact[wave, start : start + depth]
        gate_pre = acts[:, :hidden].astype(f32)
        up_pre = acts[:, hidden:].astype(f32)
        sigmoid_g = jax.nn.sigmoid(gate_pre)
        silu_g = gate_pre * sigmoid_g
        score = jnp.sum(hidden_grad * silu_g * up_pre, axis=-1).astype(jnp.bfloat16).astype(f32)
        gate_grad = hidden_grad * up_pre * sigmoid_g * (1.0 + gate_pre * (1.0 - sigmoid_g))
        up_grad = hidden_grad * silu_g
        score_high, score_low = split_in_two(score[:, None] * spreads[wave, start : start + depth])
        grads = jnp.concatenate(
            [
                gate_grad.astype(jnp.bfloat16),
                up_grad.astype(jnp.bfloat16),
                score_high,
                score_low,
                score_high,
                jnp.zeros((depth, 128 - 3 * EXPERTS), jnp.bfloat16),
            ],
            axis=1,
        )
        from_below = turned(grads, "z", 1)
        from_above = turned(grads, "z", -1)
        far = [turned(from_below[: depth // 2], "z", 1), turned(from_above[depth // 2 :], "z", -1)]
        gathered = jnp.concatenate([grads, from_above] + far + [from_below])
        back = lax.dot_general(
            gathered, back_weight, (((1,), (1,)), ((), ())), preferred_element_type=jnp.float32
        ).astype(jnp.bfloat16).reshape(side, depth, part)
        normed_grad = 0.0
        for off in (2, 1, 3, 0):
            returned = turned(pick(back, (x_at + off - z_at) % side), "x", off)
            weigh = jnp.stack([weighing(wave, source, off) for source in sources])
            normed_grad = normed_grad + jnp.einsum(
                "srt,srf->stf",
                weigh,
                returned.reshape(len(sources), CAP, part),
                preferred_element_type=f32,
            )
        return normed_grad

    second_blocks, first_out = [None] * side, [None] * side
    for sources in CHUNKS:
        blocks = [first_blocks[source] for source in sources]
        normed_grad = experts_of(0, sources, blocks)
        gained = normed_grad * gain_block
        inputs = jnp.stack([input_blocks[source] for source in sources]).astype(jnp.float32)
        factor = jnp.stack([facts[source, 0, 4] for source in sources])
        share = jnp.sum(inputs * gained, axis=-1)
        mean = sum(turned(share, "z", off) for off in range(side)) / width
        grad = (
            jnp.stack(blocks).astype(jnp.float32)
            + factor[..., None] * gained
            - inputs * (factor**3 * mean)[..., None]
        ).astype(jnp.bfloat16)
        passed = pipe_back(grad)
        for at, source in enumerate(sources):
            first_out[source] = grad[at]
            second_blocks[source] = jnp.where(is_last, last_blocks[source], passed[at])

    second_grads = [None] * side
    for sources in CHUNKS:
        normed_grad = experts_of(1, sources, [second_blocks[source] for source in sources])
        for at, source in enumerate(sources):
            second_grads[source] = normed_grad[at].astype(jnp.bfloat16)

    first_grad = gather_features(first_out)
    upstream = jnp.where(is_last, upstream_last, pipe_back(first_grad)).astype(jnp.float32)
    gained = gather_features(second_grads).astype(jnp.float32) * gain
    inputs = saved_input[1].astype(jnp.float32)
    factor = inverse[1][:, None]
    second = (
        upstream
        + factor * gained
        - inputs * factor**3 * jnp.mean(inputs * gained, axis=-1, keepdims=True)
    ).astype(jnp.bfloat16)
    return (first_grad[None], second[None])


def solution(mesh):
    side = EXPERTS
    grid = Mesh(
        mesh.devices.reshape(mesh.shape["pipe"], side, mesh.shape["expert"] // side),
        ("pipe", "x", "z"),
    )
    expert = ("x", "z")
    return jax.shard_map(
        on_device,
        mesh=grid,
        in_specs=(
            P("pipe", expert, None),
            P(expert, None),
            P("pipe", None, expert, None),
            P("pipe", None),
            P("pipe", None, None),
            P("pipe", None, expert, None),
            P("pipe", expert, None, None),
            P("pipe", expert, None, None),
            P("pipe", expert, None, None),
            P("pipe", None, expert, None, None),
        ),
        out_specs=(P("pipe", expert, None), P("pipe", expert, None)),
        check_vma=False,
    )
```

time: 745 us -> 558 us (0.75)
  the two profiles are of different devices: /device:TPU:8 before, /device:TPU:30 now
where the time goes in v1:
time: 558 us; the launch traced here: 548 us
  waiting for transfers between devices  238 us (43%)
  starting transfers between devices  123 us (22%)
  other arithmetic  71.8 us (13%)
  matrix products  57.2 us (10%)
  local copies, waits for them, and re-layouts  54.2 us (10%)
    ppermute x80, waiting for transfers between devices, turned(): lax.ppermute(value, axis, [(i, (i + offset) % count) for i in range(count)])  238 us
    ppermute x80, starting transfers between devices, turned(): lax.ppermute(value, axis, [(i, (i + offset) % count) for i in range(count)])  114 us
    dot_general x4, matrix products, experts_of(): lax.dot_general(gathered, back_weight, (((1,), (1,)), ((), ())), preferre...  27.8 us
    or x24, other arithmetic, placing(): both = matches(wave, source, expert, 0) | matches(wave, source, expert, 1)  24.4 us
    concatenate x1, local copies, waits for them, and re-layouts, on_device(): jnp.concatenate([w_gate[0, 0], w_up[0, 0], router_high, router_high, rout...  13.2 us
    unnamed x247, local copies, waits for them, and re-layouts  11.5 us
  transfers between devices with their start and end apart: 86, of which 40 were waited for; matrix products, arithmetic and copies ran while one was open for 30% of the time, Pallas kernels for 0%

profile of v1, /device:TPU:30, one launch (start us, length us, event | category | flops | bytes accessed | tf_op | source)
XLA Modules:
  0.0 548.2 jit_solution(560151585878847419)
XLA Ops:
  3.0 3.0 multiply_reduce_fusion
  7.5 4.1 collective-permute-start.5
  26.8 13.2 %concatenate.82 = bf16[1792,2176]{1,0:T(8,128)(2,1)} concatenate(bf16[1792,1024]{1,0:T(8,128)(2,1)} %bitcast.643, bf16[1792,1024]{1,0:T(8,128)(2,1)} %bitcast.644, bf16[1792,4]{1,0:T(8,128)(2,1)S(1)} %copy.87, bf16[1792,4]{1,0:T(8,128)(2,1)S(1)} %copy.87, bf16[1792,4]{1,0:T(8,128)(2,1)} %copy.89, bf16[1792,116]{1,0:T(8,128)(2,1)} %broadcast_in_dim.560), dimensions={1} | concatenate | bytes 15597568 | tf_op jit(solution)/shard_map/concatenate | solution.py:137
  64.7 2.4 collective-permute-start.14
  101.3 3.3 collective-permute-start.25
  116.5 17.1 %collective-permute-done.8 = bf16[144,1792]{1,0:T(8,128)(2,1)S(1)} collective-permute-done((bf16[144,1792]{1,0:T(8,128)(2,1)S(1)}, bf16[144,1792]{1,0:T(8,128)(2,1)S(1)}, u32[]{:S(2)}, u32[]{:S(2)}) %collective-permute-start.8) | collective-permute-done | bytes 516128 | tf_op jit(solution)/shard_map/ppermute | solution.py:19
  138.1 2.6 collective-permute-start.29
  143.2 11.8 %collective-permute-done.31 = bf16[144,1792]{1,0:T(8,128)(2,1)S(1)} collective-permute-done((bf16[144,1792]{1,0:T(8,128)(2,1)S(1)}, bf16[144,1792]{1,0:T(8,128)(2,1)S(1)}, u32[]{:S(2)}, u32[]{:S(2)}) %collective-permute-start.31) | collective-permute-done | bytes 516128 | tf_op jit(solution)/shard_map/ppermute | solution.py:19
  164.8 5.0 collective-permute-done.9
  171.4 3.5 collective-permute-done.34
  175.6 5.7 %collective-permute-done.32 = bf16[144,512]{1,0:T(8,128)(2,1)S(1)} collective-permute-done((bf16[144,512]{1,0:T(8,128)(2,1)S(1)}, bf16[144,512]{1,0:T(8,128)(2,1)S(1)}, u32[]{:S(2)}, u32[]{:S(2)}) %collective-permute-start.32) | collective-permute-done | bytes 147488 | tf_op jit(solution)/shard_map/ppermute | solution.py:19
  183.5 3.0 collective-permute-start.35
  188.7 2.8 collective-permute-done.10
  191.9 2.9 collective-permute-done.33
  211.7 8.3 %collective-permute-done.17 = bf16[144,2176]{1,0:T(8,128)(2,1)} collective-permute-done((bf16[144,2176]{1,0:T(8,128)(2,1)}, bf16[144,2176]{1,0:T(8,128)(2,1)}, u32[]{:S(2)}, u32[]{:S(2)}) %collective-permute-start.17) | collective-permute-done | bytes 626720 | tf_op jit(solution)/shard_map/ppermute | solution.py:19
  222.8 15.5 %collective-permute-done.37 = bf16[144,2176]{1,0:T(8,128)(2,1)S(1)} collective-permute-done((bf16[144,2176]{1,0:T(8,128)(2,1)}, bf16[144,2176]{1,0:T(8,128)(2,1)S(1)}, u32[]{:S(2)}, u32[]{:S(2)}) %collective-permute-start.37) | collective-permute-done | bytes 626720 | tf_op jit(solution)/shard_map/ppermute | solution.py:19
  246.8 8.6 %convolution_convert_fusion.3 = bf16[576,1792]{1,0:T(8,128)(2,1)S(1)} fusion(bf16[576,2176]{1,0:T(8,128)(2,1)S(1)} %constant_dynamic-update-slice_fusion, bf16[1792,2176]{1,0:T(8,128)(2,1)} %concatenate.82), kind=kOutput, calls=%fused_computation.19 | convolution fusion | flops 4493131776 | bytes 12369920 | tf_op jit(solution)/shard_map/dot_general | solution.py:241
  255.8 5.3 convolution_convert_fusion.2
  261.4 3.3 collective-permute-start.41
  265.6 12.5 %collective-permute-done.42 = bf16[144,1792]{1,0:T(8,128)(2,1)S(1)} collective-permute-done((bf16[144,1792]{1,0:T(8,128)(2,1)S(1)}, bf16[144,1792]{1,0:T(8,128)(2,1)S(1)}, u32[]{:S(2)}, u32[]{:S(2)}) %collective-permute-start.42) | collective-permute-done | bytes 516128 | tf_op jit(solution)/shard_map/ppermute | solution.py:19
  282.2 10.4 %collective-permute-done.40 = bf16[144,1792]{1,0:T(8,128)(2,1)S(1)} collective-permute-done((bf16[144,1792]{1,0:T(8,128)(2,1)S(1)}, bf16[144,1792]{1,0:T(8,128)(2,1)S(1)}, u32[]{:S(2)}, u32[]{:S(2)}) %collective-permute-start.40) | collective-permute-done | bytes 516128 | tf_op jit(solution)/shard_map/ppermute | solution.py:19
  292.6 3.5 collective-permute-start.20
  297.0 4.9 collective-permute-start.45
  306.9 7.0 %collective-permute-start.43 = (f32[2,128]{1,0:T(2,128)S(1)}, f32[2,128]{1,0:T(2,128)S(1)}, u32[]{:S(2)}, u32[]{:S(2)}) collective-permute-start(f32[2,128]{1,0:T(2,128)S(1)} %get-tuple-element.438), channel_id=1, source_target_pairs={{0,1},{1,2},{2,3},{3,0},{4,5},{5,6},{6,7},{7,4},{8,9},{9,10},{10,1... | collective-permute-start | bytes 3080 | tf_op jit(solution)/shard_map/ppermute | solution.py:19
  325.5 2.5 collective-permute-start.48
  331.7 16.7 %collective-permute-done.48 = bf16[128,1792]{1,0:T(8,128)(2,1)S(1)} collective-permute-done((bf16[128,1792]{1,0:T(8,128)(2,1)S(1)}, bf16[128,1792]{1,0:T(8,128)(2,1)S(1)}, u32[]{:S(2)}, u32[]{:S(2)}) %collective-permute-start.48) | collective-permute-done | bytes 458784 | tf_op jit(solution)/shard_map/ppermute | solution.py:19
  348.4 3.7 collective-permute-done.46
  353.9 5.2 collective-permute-start.55
  359.9 2.5 collective-permute-start.71
  363.7 6.5 %collective-permute-done.56 = bf16[144,1792]{1,0:T(8,128)(2,1)S(1)} collective-permute-done((bf16[144,1792]{1,0:T(8,128)(2,1)S(1)}, bf16[144,1792]{1,0:T(8,128)(2,1)S(1)}, u32[]{:S(2)}, u32[]{:S(2)}) %collective-permute-start.56) | collective-permute-done | bytes 516128 | tf_op jit(solution)/shard_map/ppermute | solution.py:19
  371.9 10.5 %collective-permute-done.55 = bf16[144,1792]{1,0:T(8,128)(2,1)S(1)} collective-permute-done((bf16[144,1792]{1,0:T(8,128)(2,1)S(1)}, bf16[144,1792]{1,0:T(8,128)(2,1)S(1)}, u32[]{:S(2)}, u32[]{:S(2)}) %collective-permute-start.55) | collective-permute-done | bytes 516128 | tf_op jit(solution)/shard_map/ppermute | solution.py:19
  387.0 4.3 collective-permute-done.71
  391.3 12.3 %collective-permute-done.70 = bf16[144,1792]{1,0:T(8,128)(2,1)S(1)} collective-permute-done((bf16[144,1792]{1,0:T(8,128)(2,1)S(1)}, bf16[144,1792]{1,0:T(8,128)(2,1)S(1)}, u32[]{:S(2)}, u32[]{:S(2)}) %collective-permute-start.70) | collective-permute-done | bytes 516128 | tf_op jit(solution)/shard_map/ppermute | solution.py:19
  419.5 4.3 collective-permute-done.75
  433.4 13.2 %collective-permute-done.62 = bf16[144,2176]{1,0:T(8,128)(2,1)} collective-permute-done((bf16[144,2176]{1,0:T(8,128)(2,1)S(1)}, bf16[144,2176]{1,0:T(8,128)(2,1)}, u32[]{:S(2)}, u32[]{:S(2)}) %collective-permute-start.62) | collective-permute-done | bytes 626720 | tf_op jit(solution)/shard_map/ppermute | solution.py:19
  449.1 3.0 collective-permute-start.64
  452.1 7.8 %collective-permute-done.77 = bf16[144,2176]{1,0:T(8,128)(2,1)S(1)} collective-permute-done((bf16[144,2176]{1,0:T(8,128)(2,1)S(1)}, bf16[144,2176]{1,0:T(8,128)(2,1)S(1)}, u32[]{:S(2)}, u32[]{:S(2)}) %collective-permute-start.77) | collective-permute-done | bytes 626720 | tf_op jit(solution)/shard_map/ppermute | solution.py:19
  460.4 3.0 collective-permute-start.79
  468.0 8.6 %convolution_convert_fusion.1 = bf16[576,1792]{1,0:T(8,128)(2,1)S(1)} fusion(bf16[576,2176]{1,0:T(8,128)(2,1)S(1)} %constant_dynamic-update-slice_fusion.10, bf16[1792,2176]{1,0:T(8,128)(2,1)} %concatenate.82), kind=kOutput, calls=%fused_computation.17 | convolution fusion | flops 4493131776 | bytes 12369920 | tf_op jit(solution)/shard_map/dot_general | solution.py:241
  477.6 2.5 collective-permute-start.66
  481.7 5.3 convolution_convert_fusion
  489.6 7.9 %collective-permute-done.67 = bf16[144,1792]{1,0:T(8,128)(2,1)S(1)} collective-permute-done((bf16[144,1792]{1,0:T(8,128)(2,1)S(1)}, bf16[144,1792]{1,0:T(8,128)(2,1)S(1)}, u32[]{:S(2)}, u32[]{:S(2)}) %collective-permute-start.67) | collective-permute-done | bytes 516128 | tf_op jit(solution)/shard_map/ppermute | solution.py:19
  500.4 13.6 %collective-permute-done.82 = bf16[144,1792]{1,0:T(8,128)(2,1)S(1)} collective-permute-done((bf16[144,1792]{1,0:T(8,128)(2,1)S(1)}, bf16[144,1792]{1,0:T(8,128)(2,1)S(1)}, u32[]{:S(2)}, u32[]{:S(2)}) %collective-permute-start.82) | collective-permute-done | bytes 516128 | tf_op jit(solution)/shard_map/ppermute | solution.py:19
  514.5 5.2 collective-permute-done.81
  525.0 9.1 %collective-permute-done.85 = bf16[128,1792]{1,0:T(8,128)(2,1)S(1)} collective-permute-done((bf16[128,1792]{1,0:T(8,128)(2,1)S(1)}, bf16[128,1792]{1,0:T(8,128)(2,1)S(1)}, u32[]{:S(2)}, u32[]{:S(2)}) %collective-permute-start.85) | collective-permute-done | bytes 458784 | tf_op jit(solution)/shard_map/ppermute | solution.py:19
  534.0 2.7 collective-permute-done.84
  536.8 4.6 collective-permute-done.83
  544.4 3.6 fusion.58
  (625 shorter events, 226.6 us)
Async XLA Ops:
  7.5 32.5 %collective-permute-start.5 = (f32[2,16,128]{2,1,0:T(8,128)S(1)}, f32[2,16,128]{2,1,0:T(8,128)S(1)}, u32[]{:S(2)}, u32[]{:S(2)}) collective-permute-start(f32[2,16,128]{2,1,0:T(8,128)S(1)} %bitcast.688), channel_id=1, source_target_pairs={{0,3},{1,0},{2,1},{3,2},{4,7},{5,4},{6,5},{7,6},{8,11},{9,8},{10,9... | collective-permute-start | bytes 49160 | tf_op jit(solution)/shard_map/ppermute | solution.py:19
  11.6 28.5 %collective-permute-start.4 = (f32[2,16,128]{2,1,0:T(8,128)S(1)}, f32[2,16,128]{2,1,0:T(8,128)S(1)}, u32[]{:S(2)}, u32[]{:S(2)}) collective-permute-start(f32[2,16,128]{2,1,0:T(8,128)S(1)} %bitcast.689), channel_id=1, source_target_pairs={{0,2},{1,3},{2,0},{3,1},{4,6},{5,7},{6,4},{7,5},{8,10},{9,11},{10,... | collective-permute-start | bytes 49160 | tf_op jit(solution)/shard_map/ppermute | solution.py:19
  11.6 28.5 %collective-permute-start.3 = (f32[2,16,128]{2,1,0:T(8,128)S(1)}, f32[2,16,128]{2,1,0:T(8,128)S(1)}, u32[]{:S(2)}, u32[]{:S(2)}) collective-permute-start(f32[2,16,128]{2,1,0:T(8,128)S(1)} %bitcast.690), channel_id=1, source_target_pairs={{0,1},{1,2},{2,3},{3,0},{4,5},{5,6},{6,7},{7,4},{8,9},{9,10},{10,1... | collective-permute-start | bytes 49160 | tf_op jit(solution)/shard_map/ppermute | solution.py:19
  14.0 93.3 %collective-permute-start.2 = (bf16[128,1792]{1,0:T(8,128)(2,1)}, bf16[128,1792]{1,0:T(8,128)(2,1)}, u32[]{:S(2)}, u32[]{:S(2)}) collective-permute-start(bf16[128,1792]{1,0:T(8,128)(2,1)} %get-tuple-element.120), channel_id=1, source_target_pairs={{0,3},{1,0},{2,1},{3,2},{4,7},{5,4},{6,5},{7,6},{8,11},{9,8},{10,9... | collective-permute-start | bytes 1376264 | tf_op jit(solution)/shard_map/ppermute | solution.py:19
  16.0 91.3 %collective-permute-start.1 = (bf16[128,1792]{1,0:T(8,128)(2,1)}, bf16[128,1792]{1,0:T(8,128)(2,1)}, u32[]{:S(2)}, u32[]{:S(2)}) collective-permute-start(bf16[128,1792]{1,0:T(8,128)(2,1)} %get-tuple-element.121), channel_id=1, source_target_pairs={{0,2},{1,3},{2,0},{3,1},{4,6},{5,7},{6,4},{7,5},{8,10},{9,11},{10,... | collective-permute-start | bytes 1376264 | tf_op jit(solution)/shard_map/ppermute | solution.py:19
  40.0 67.3 %collective-permute-start = (bf16[128,1792]{1,0:T(8,128)(2,1)}, bf16[128,1792]{1,0:T(8,128)(2,1)}, u32[]{:S(2)}, u32[]{:S(2)}) collective-permute-start(bf16[128,1792]{1,0:T(8,128)(2,1)} %get-tuple-element.119), channel_id=1, source_target_pairs={{0,1},{1,2},{2,3},{3,0},{4,5},{5,6},{6,7},{7,4},{8,9},{9,10},{10,1... | collective-permute-start | bytes 1376264 | tf_op jit(solution)/shard_map/ppermute | solution.py:19
  54.5 45.6 %collective-permute-start.13 = (f32[2,288,4]{1,2,0:T(4,128)}, f32[2,288,4]{1,2,0:T(4,128)}, u32[]{:S(2)}, u32[]{:S(2)}) collective-permute-start(f32[2,288,4]{1,2,0:T(4,128)} %reshape.8426), channel_id=1, source_target_pairs={{0,4},{4,8},{8,12},{12,0},{1,5},{5,9},{9,13},{13,1},{2,6},{6,10},{... | collective-permute-start | bytes 27656 | tf_op jit(solution)/shard_map/ppermute | solution.py:19
  64.7 36.5 %collective-permute-start.14 = (f32[2,288,4]{1,2,0:T(4,128)}, f32[2,288,4]{1,2,0:T(4,128)}, u32[]{:S(2)}, u32[]{:S(2)}) collective-permute-start(f32[2,288,4]{1,2,0:T(4,128)} %reshape.8427), channel_id=1, source_target_pairs={{0,8},{4,12},{8,0},{12,4},{1,9},{5,13},{9,1},{13,5},{2,10},{6,14},... | collective-permute-start | bytes 27656 | tf_op jit(solution)/shard_map/ppermute | solution.py:19
  101.3 81.8 %collective-permute-start.25 = (bf16[128,1792]{1,0:T(8,128)(2,1)}, bf16[128,1792]{1,0:T(8,128)(2,1)S(1)}, u32[]{:S(2)}, u32[]{:S(2)}) collective-permute-start(bf16[128,1792]{1,0:T(8,128)(2,1)} %get-tuple-element.115), channel_id=1, source_target_pairs={{0,3},{1,0},{2,1},{3,2},{4,7},{5,4},{6,5},{7,6},{8,11},{9,8},{10,9... | collective-permute-start | bytes 1376264 | tf_op jit(solution)/shard_map/ppermute | solution.py:19
  105.0 78.5 %collective-permute-start.24 = (bf16[128,1792]{1,0:T(8,128)(2,1)S(1)}, bf16[128,1792]{1,0:T(8,128)(2,1)S(1)}, u32[]{:S(2)}, u32[]{:S(2)}) collective-permute-start(bf16[128,1792]{1,0:T(8,128)(2,1)S(1)} %copy-done.23), channel_id=1, source_target_pairs={{0,2},{1,3},{2,0},{3,1},{4,6},{5,7},{6,4},{7,5},{8,10},{9,11},{10,... | collective-permute-start | bytes 1376264 | tf_op jit(solution)/shard_map/ppermute | solution.py:19
  109.9 23.7 %collective-permute-start.8 = (bf16[144,1792]{1,0:T(8,128)(2,1)S(1)}, bf16[144,1792]{1,0:T(8,128)(2,1)S(1)}, u32[]{:S(2)}, u32[]{:S(2)}) collective-permute-start(bf16[144,1792]{1,0:T(8,128)(2,1)S(1)} %bitcast.710), channel_id=1, source_target_pairs={{0,12},{4,0},{8,4},{12,8},{1,13},{5,1},{9,5},{13,9},{2,14},{6,2},{... | collective-permute-start | bytes 1548296 | tf_op jit(solution)/shard_map/ppermute | solution.py:19
  110.3 25.6 %collective-permute-start.7 = (bf16[144,1792]{1,0:T(8,128)(2,1)S(1)}, bf16[144,1792]{1,0:T(8,128)(2,1)S(1)}, u32[]{:S(2)}, u32[]{:S(2)}) collective-permute-start(bf16[144,1792]{1,0:T(8,128)(2,1)S(1)} %bitcast.711), channel_id=1, source_target_pairs={{0,8},{4,12},{8,0},{12,4},{1,9},{5,13},{9,1},{13,5},{2,10},{6,14},... | collective-permute-start | bytes 1548296 | tf_op jit(solution)/shard_map/ppermute | solution.py:19
  112.9 25.3 %collective-permute-start.6 = (bf16[144,1792]{1,0:T(8,128)(2,1)S(1)}, bf16[144,1792]{1,0:T(8,128)(2,1)S(1)}, u32[]{:S(2)}, u32[]{:S(2)}) collective-permute-start(bf16[144,1792]{1,0:T(8,128)(2,1)S(1)} %bitcast.712), channel_id=1, source_target_pairs={{0,4},{4,8},{8,12},{12,0},{1,5},{5,9},{9,13},{13,1},{2,6},{6,10},{... | collective-permute-start | bytes 1548296 | tf_op jit(solution)/shard_map/ppermute | solution.py:19
  133.6 21.4 %collective-permute-start.31 = (bf16[144,1792]{1,0:T(8,128)(2,1)S(1)}, bf16[144,1792]{1,0:T(8,128)(2,1)S(1)}, u32[]{:S(2)}, u32[]{:S(2)}) collective-permute-start(bf16[144,1792]{1,0:T(8,128)(2,1)S(1)} %bitcast.708), channel_id=1, source_target_pairs={{0,12},{4,0},{8,4},{12,8},{1,13},{5,1},{9,5},{13,9},{2,14},{6,2},{... | collective-permute-start | bytes 1548296 | tf_op jit(solution)/shard_map/ppermute | solution.py:19
  135.9 20.9 %collective-permute-start.30 = (bf16[144,1792]{1,0:T(8,128)(2,1)S(1)}, bf16[144,1792]{1,0:T(8,128)(2,1)S(1)}, u32[]{:S(2)}, u32[]{:S(2)}) collective-permute-start(bf16[144,1792]{1,0:T(8,128)(2,1)S(1)} %bitcast.706), channel_id=1, source_target_pairs={{0,8},{4,12},{8,0},{12,4},{1,9},{5,13},{9,1},{13,5},{2,10},{6,14},... | collective-permute-start | bytes 1548296 | tf_op jit(solution)/shard_map/ppermute | solution.py:19
  155.0 31.5 %collective-permute-start.23 = (bf16[128,1792]{1,0:T(8,128)(2,1)S(1)}, bf16[128,1792]{1,0:T(8,128)(2,1)S(1)}, u32[]{:S(2)}, u32[]{:S(2)}) collective-permute-start(bf16[128,1792]{1,0:T(8,128)(2,1)S(1)} %copy-done.22), channel_id=1, source_target_pairs={{0,1},{1,2},{2,3},{3,0},{4,5},{5,6},{6,7},{7,4},{8,9},{9,10},{10,1... | collective-permute-start | bytes 1376264 | tf_op jit(solution)/shard_map/ppermute | solution.py:19
  156.9 168.7 %collective-permute-start.52 = (bf16[128,1792]{1,0:T(8,128)(2,1)}, bf16[128,1792]{1,0:T(8,128)(2,1)}, u32[]{:S(2)}, u32[]{:S(2)}) collective-permute-start(bf16[128,1792]{1,0:T(8,128)(2,1)} %get-tuple-element.96), channel_id=1, source_target_pairs={{112,115},{113,112},{114,113},{115,114},{116,119},{117,116},{118,1... | collective-permute-start | bytes 1376264 | tf_op jit(solution)/shard_map/ppermute | solution.py:126
  200.7 21.0 %collective-permute-start.16 = (bf16[144,2176]{1,0:T(8,128)(2,1)}, bf16[144,2176]{1,0:T(8,128)(2,1)}, u32[]{:S(2)}, u32[]{:S(2)}) collective-permute-start(bf16[144,2176]{1,0:T(8,128)(2,1)} %concatenate.80), channel_id=1, source_target_pairs={{0,3},{1,0},{2,1},{3,2},{4,7},{5,4},{6,5},{7,6},{8,11},{9,8},{10,9... | collective-permute-start | bytes 1880072 | tf_op jit(solution)/shard_map/ppermute | solution.py:19
  207.5 32.0 %collective-permute-start.36 = (bf16[144,2176]{1,0:T(8,128)(2,1)}, bf16[144,2176]{1,0:T(8,128)(2,1)S(1)}, u32[]{:S(2)}, u32[]{:S(2)}) collective-permute-start(bf16[144,2176]{1,0:T(8,128)(2,1)} %concatenate.86), channel_id=1, source_target_pairs={{0,3},{1,0},{2,1},{3,2},{4,7},{5,4},{6,5},{7,6},{8,11},{9,8},{10,9... | collective-permute-start | bytes 1880072 | tf_op jit(solution)/shard_map/ppermute | solution.py:19
  209.4 28.9 %collective-permute-start.37 = (bf16[144,2176]{1,0:T(8,128)(2,1)}, bf16[144,2176]{1,0:T(8,128)(2,1)S(1)}, u32[]{:S(2)}, u32[]{:S(2)}) collective-permute-start(bf16[144,2176]{1,0:T(8,128)(2,1)} %concatenate.86), channel_id=1, source_target_pairs={{0,1},{1,2},{2,3},{3,0},{4,5},{5,6},{6,7},{7,4},{8,9},{9,10},{10,1... | collective-permute-start | bytes 1880072 | tf_op jit(solution)/shard_map/ppermute | solution.py:19
  220.0 108.1 %collective-permute-start.51 = (bf16[128,1792]{1,0:T(8,128)(2,1)S(1)}, bf16[128,1792]{1,0:T(8,128)(2,1)S(1)}, u32[]{:S(2)}, u32[]{:S(2)}) collective-permute-start(bf16[128,1792]{1,0:T(8,128)(2,1)S(1)} %copy-done.21), channel_id=1, source_target_pairs={{112,114},{113,115},{114,112},{115,113},{116,118},{117,119},{118,1... | collective-permute-start | bytes 1376264 | tf_op jit(solution)/shard_map/ppermute | solution.py:126
  221.7 21.4 %collective-permute-start.18 = (bf16[72,2176]{1,0:T(8,128)(2,1)S(1)}, bf16[72,2176]{1,0:T(8,128)(2,1)S(1)}, u32[]{:S(2)}, u32[]{:S(2)}) collective-permute-start(bf16[72,2176]{1,0:T(8,128)(2,1)S(1)} %slice.328), channel_id=1, source_target_pairs={{0,1},{1,2},{2,3},{3,0},{4,5},{5,6},{6,7},{7,4},{8,9},{9,10},{10,1... | collective-permute-start | bytes 940040 | tf_op jit(solution)/shard_map/ppermute | solution.py:19
  255.5 41.5 %collective-permute-start.22 = (bf16[144,1792]{1,0:T(8,128)(2,1)S(1)}, bf16[144,1792]{1,0:T(8,128)(2,1)S(1)}, u32[]{:S(2)}, u32[]{:S(2)}) collective-permute-start(bf16[144,1792]{1,0:T(8,128)(2,1)S(1)} %get-tuple-element.80), channel_id=1, source_target_pairs={{0,12},{4,0},{8,4},{12,8},{1,13},{5,1},{9,5},{13,9},{2,14},{6,2},{... | collective-permute-start | bytes 1548296 | tf_op jit(solution)/shard_map/ppermute | solution.py:19
  280.6 23.9 %collective-permute-start.21 = (bf16[144,1792]{1,0:T(8,128)(2,1)S(1)}, bf16[144,1792]{1,0:T(8,128)(2,1)S(1)}, u32[]{:S(2)}, u32[]{:S(2)}) collective-permute-start(bf16[144,1792]{1,0:T(8,128)(2,1)S(1)} %get-tuple-element.81), channel_id=1, source_target_pairs={{0,4},{4,8},{8,12},{12,0},{1,5},{5,9},{9,13},{13,1},{2,6},{6,10},{... | collective-permute-start | bytes 1548296 | tf_op jit(solution)/shard_map/ppermute | solution.py:19
  320.2 32.3 %collective-permute-start.68 = (bf16[2,128,1792]{2,1,0:T(8,128)(2,1)S(1)}, bf16[2,128,1792]{2,1,0:T(8,128)(2,1)S(1)}, u32[]{:S(2)}, u32[]{:S(2)}) collective-permute-start(bf16[2,128,1792]{2,1,0:T(8,128)(2,1)S(1)} %fusion.57), channel_id=1, source_target_pairs={{16,0},{32,16},{48,32},{64,48},{80,64},{96,80},{112,96},{17,1},{33... | collective-permute-start | bytes 2752520 | tf_op jit(solution)/shard_map/ppermute | solution.py:115
  322.8 29.7 %collective-permute-start.53 = (bf16[2,128,1792]{2,1,0:T(8,128)(2,1)S(1)}, bf16[2,128,1792]{2,1,0:T(8,128)(2,1)S(1)}, u32[]{:S(2)}, u32[]{:S(2)}) collective-permute-start(bf16[2,128,1792]{2,1,0:T(8,128)(2,1)S(1)} %fusion.54), channel_id=1, source_target_pairs={{16,0},{32,16},{48,32},{64,48},{80,64},{96,80},{112,96},{17,1},{33... | collective-permute-start | bytes 2752520 | tf_op jit(solution)/shard_map/ppermute | solution.py:115
  325.5 22.9 %collective-permute-start.48 = (bf16[128,1792]{1,0:T(8,128)(2,1)S(1)}, bf16[128,1792]{1,0:T(8,128)(2,1)S(1)}, u32[]{:S(2)}, u32[]{:S(2)}) collective-permute-start(bf16[128,1792]{1,0:T(8,128)(2,1)S(1)} %get-tuple-element.105), channel_id=1, source_target_pairs={{0,3},{1,0},{2,1},{3,2},{4,7},{5,4},{6,5},{7,6},{8,11},{9,8},{10,9... | collective-permute-start | bytes 1376264 | tf_op jit(solution)/shard_map/ppermute | solution.py:19
  328.1 20.4 %collective-permute-start.47 = (bf16[128,1792]{1,0:T(8,128)(2,1)S(1)}, bf16[128,1792]{1,0:T(8,128)(2,1)S(1)}, u32[]{:S(2)}, u32[]{:S(2)}) collective-permute-start(bf16[128,1792]{1,0:T(8,128)(2,1)S(1)} %get-tuple-element.104), channel_id=1, source_target_pairs={{0,2},{1,3},{2,0},{3,1},{4,6},{5,7},{6,4},{7,5},{8,10},{9,11},{10,... | collective-permute-start | bytes 1376264 | tf_op jit(solution)/shard_map/ppermute | solution.py:19
  329.5 22.6 %collective-permute-start.46 = (bf16[128,1792]{1,0:T(8,128)(2,1)S(1)}, bf16[128,1792]{1,0:T(8,128)(2,1)S(1)}, u32[]{:S(2)}, u32[]{:S(2)}) collective-permute-start(bf16[128,1792]{1,0:T(8,128)(2,1)S(1)} %get-tuple-element.103), channel_id=1, source_target_pairs={{0,1},{1,2},{2,3},{3,0},{4,5},{5,6},{6,7},{7,4},{8,9},{9,10},{10,1... | collective-permute-start | bytes 1376264 | tf_op jit(solution)/shard_map/ppermute | solution.py:19
  353.9 28.5 %collective-permute-start.55 = (bf16[144,1792]{1,0:T(8,128)(2,1)S(1)}, bf16[144,1792]{1,0:T(8,128)(2,1)S(1)}, u32[]{:S(2)}, u32[]{:S(2)}) collective-permute-start(bf16[144,1792]{1,0:T(8,128)(2,1)S(1)} %bitcast.705), channel_id=1, source_target_pairs={{0,8},{4,12},{8,0},{12,4},{1,9},{5,13},{9,1},{13,5},{2,10},{6,14},... | collective-permute-start | bytes 1548296 | tf_op jit(solution)/shard_map/ppermute | solution.py:19
  359.4 23.0 %collective-permute-start.54 = (bf16[144,1792]{1,0:T(8,128)(2,1)S(1)}, bf16[144,1792]{1,0:T(8,128)(2,1)S(1)}, u32[]{:S(2)}, u32[]{:S(2)}) collective-permute-start(bf16[144,1792]{1,0:T(8,128)(2,1)S(1)} %bitcast.709), channel_id=1, source_target_pairs={{0,4},{4,8},{8,12},{12,0},{1,5},{5,9},{9,13},{13,1},{2,6},{6,10},{... | collective-permute-start | bytes 1548296 | tf_op jit(solution)/shard_map/ppermute | solution.py:19
  359.9 31.5 %collective-permute-start.71 = (bf16[144,1792]{1,0:T(8,128)(2,1)S(1)}, bf16[144,1792]{1,0:T(8,128)(2,1)S(1)}, u32[]{:S(2)}, u32[]{:S(2)}) collective-permute-start(bf16[144,1792]{1,0:T(8,128)(2,1)S(1)} %bitcast.701), channel_id=1, source_target_pairs={{0,12},{4,0},{8,4},{12,8},{1,13},{5,1},{9,5},{13,9},{2,14},{6,2},{... | collective-permute-start | bytes 1548296 | tf_op jit(solution)/shard_map/ppermute | solution.py:19
  362.6 41.0 %collective-permute-start.70 = (bf16[144,1792]{1,0:T(8,128)(2,1)S(1)}, bf16[144,1792]{1,0:T(8,128)(2,1)S(1)}, u32[]{:S(2)}, u32[]{:S(2)}) collective-permute-start(bf16[144,1792]{1,0:T(8,128)(2,1)S(1)} %bitcast.702), channel_id=1, source_target_pairs={{0,8},{4,12},{8,0},{12,4},{1,9},{5,13},{9,1},{13,5},{2,10},{6,14},... | collective-permute-start | bytes 1548296 | tf_op jit(solution)/shard_map/ppermute | solution.py:19
  370.2 33.4 %collective-permute-start.69 = (bf16[144,1792]{1,0:T(8,128)(2,1)S(1)}, bf16[144,1792]{1,0:T(8,128)(2,1)S(1)}, u32[]{:S(2)}, u32[]{:S(2)}) collective-permute-start(bf16[144,1792]{1,0:T(8,128)(2,1)S(1)} %bitcast.707), channel_id=1, source_target_pairs={{0,4},{4,8},{8,12},{12,0},{1,5},{5,9},{9,13},{13,1},{2,6},{6,10},{... | collective-permute-start | bytes 1548296 | tf_op jit(solution)/shard_map/ppermute | solution.py:19
  384.9 23.4 %collective-permute-start.59 = (bf16[144,512]{1,0:T(8,128)(2,1)S(1)}, bf16[144,512]{1,0:T(8,128)(2,1)S(1)}, u32[]{:S(2)}, u32[]{:S(2)}) collective-permute-start(bf16[144,512]{1,0:T(8,128)(2,1)S(1)} %get-tuple-element.137), channel_id=1, source_target_pairs={{0,3},{1,0},{2,1},{3,2},{4,7},{5,4},{6,5},{7,6},{8,11},{9,8},{10,9... | collective-permute-start | bytes 442376 | tf_op jit(solution)/shard_map/ppermute | solution.py:19
  385.6 24.0 %collective-permute-start.57 = (bf16[144,512]{1,0:T(8,128)(2,1)S(1)}, bf16[144,512]{1,0:T(8,128)(2,1)S(1)}, u32[]{:S(2)}, u32[]{:S(2)}) collective-permute-start(bf16[144,512]{1,0:T(8,128)(2,1)S(1)} %get-tuple-element.136), channel_id=1, source_target_pairs={{0,1},{1,2},{2,3},{3,0},{4,5},{5,6},{6,7},{7,4},{8,9},{9,10},{10,1... | collective-permute-start | bytes 442376 | tf_op jit(solution)/shard_map/ppermute | solution.py:19
  417.4 126.9 %collective-permute-start.49 = (bf16[128,7168]{1,0:T(8,128)(2,1)}, bf16[128,7168]{1,0:T(8,128)(2,1)}, u32[]{:S(2)}, u32[]{:S(2)}) collective-permute-start(bf16[128,7168]{1,0:T(8,128)(2,1)} %get-tuple-element.82), channel_id=1, source_target_pairs={{16,0},{32,16},{48,32},{64,48},{80,64},{96,80},{112,96},{17,1},{33... | collective-permute-start | bytes 5505032 | tf_op jit(solution)/shard_map/ppermute | solution.py:115
  427.7 20.5 %collective-permute-start.61 = (bf16[144,2176]{1,0:T(8,128)(2,1)S(1)}, bf16[144,2176]{1,0:T(8,128)(2,1)}, u32[]{:S(2)}, u32[]{:S(2)}) collective-permute-start(bf16[144,2176]{1,0:T(8,128)(2,1)S(1)} %concatenate.92), channel_id=1, source_target_pairs={{0,3},{1,0},{2,1},{3,2},{4,7},{5,4},{6,5},{7,6},{8,11},{9,8},{10,9... | collective-permute-start | bytes 1880072 | tf_op jit(solution)/shard_map/ppermute | solution.py:19
  431.2 29.1 %collective-permute-start.76 = (bf16[144,2176]{1,0:T(8,128)(2,1)S(1)}, bf16[144,2176]{1,0:T(8,128)(2,1)S(1)}, u32[]{:S(2)}, u32[]{:S(2)}) collective-permute-start(bf16[144,2176]{1,0:T(8,128)(2,1)S(1)} %concatenate.97), channel_id=1, source_target_pairs={{0,3},{1,0},{2,1},{3,2},{4,7},{5,4},{6,5},{7,6},{8,11},{9,8},{10,9... | collective-permute-start | bytes 1880072 | tf_op jit(solution)/shard_map/ppermute | solution.py:19
  432.9 27.0 %collective-permute-start.77 = (bf16[144,2176]{1,0:T(8,128)(2,1)S(1)}, bf16[144,2176]{1,0:T(8,128)(2,1)S(1)}, u32[]{:S(2)}, u32[]{:S(2)}) collective-permute-start(bf16[144,2176]{1,0:T(8,128)(2,1)S(1)} %concatenate.97), channel_id=1, source_target_pairs={{0,1},{1,2},{2,3},{3,0},{4,5},{5,6},{6,7},{7,4},{8,9},{9,10},{10,1... | collective-permute-start | bytes 1880072 | tf_op jit(solution)/shard_map/ppermute | solution.py:19
  459.9 20.2 %collective-permute-start.78 = (bf16[72,2176]{1,0:T(8,128)(2,1)S(1)}, bf16[72,2176]{1,0:T(8,128)(2,1)S(1)}, u32[]{:S(2)}, u32[]{:S(2)}) collective-permute-start(bf16[72,2176]{1,0:T(8,128)(2,1)S(1)} %slice.702), channel_id=1, source_target_pairs={{0,1},{1,2},{2,3},{3,0},{4,5},{5,6},{6,7},{7,4},{8,9},{9,10},{10,1... | collective-permute-start | bytes 940040 | tf_op jit(solution)/shard_map/ppermute | solution.py:19
  460.4 21.1 %collective-permute-start.79 = (bf16[72,2176]{1,0:T(8,128)(2,1)S(1)}, bf16[72,2176]{1,0:T(8,128)(2,1)S(1)}, u32[]{:S(2)}, u32[]{:S(2)}) collective-permute-start(bf16[72,2176]{1,0:T(8,128)(2,1)S(1)} %slice.703), channel_id=1, source_target_pairs={{0,3},{1,0},{2,1},{3,2},{4,7},{5,4},{6,5},{7,6},{8,11},{9,8},{10,9... | collective-permute-start | bytes 940040 | tf_op jit(solution)/shard_map/ppermute | solution.py:19
  476.8 20.6 %collective-permute-start.67 = (bf16[144,1792]{1,0:T(8,128)(2,1)S(1)}, bf16[144,1792]{1,0:T(8,128)(2,1)S(1)}, u32[]{:S(2)}, u32[]{:S(2)}) collective-permute-start(bf16[144,1792]{1,0:T(8,128)(2,1)S(1)} %get-tuple-element.72), channel_id=1, source_target_pairs={{0,12},{4,0},{8,4},{12,8},{1,13},{5,1},{9,5},{13,9},{2,14},{6,2},{... | collective-permute-start | bytes 1548296 | tf_op jit(solution)/shard_map/ppermute | solution.py:19
  477.6 22.4 %collective-permute-start.66 = (bf16[144,1792]{1,0:T(8,128)(2,1)S(1)}, bf16[144,1792]{1,0:T(8,128)(2,1)S(1)}, u32[]{:S(2)}, u32[]{:S(2)}) collective-permute-start(bf16[144,1792]{1,0:T(8,128)(2,1)S(1)} %get-tuple-element.73), channel_id=1, source_target_pairs={{0,4},{4,8},{8,12},{12,0},{1,5},{5,9},{9,13},{13,1},{2,6},{6,10},{... | collective-permute-start | bytes 1548296 | tf_op jit(solution)/shard_map/ppermute | solution.py:19
  480.1 40.0 %collective-permute-start.65 = (bf16[144,1792]{1,0:T(8,128)(2,1)S(1)}, bf16[144,1792]{1,0:T(8,128)(2,1)S(1)}, u32[]{:S(2)}, u32[]{:S(2)}) collective-permute-start(bf16[144,1792]{1,0:T(8,128)(2,1)S(1)} %get-tuple-element.70), channel_id=1, source_target_pairs={{0,8},{4,12},{8,0},{12,4},{1,9},{5,13},{9,1},{13,5},{2,10},{6,14},... | collective-permute-start | bytes 1548296 | tf_op jit(solution)/shard_map/ppermute | solution.py:19
  487.1 26.9 %collective-permute-start.82 = (bf16[144,1792]{1,0:T(8,128)(2,1)S(1)}, bf16[144,1792]{1,0:T(8,128)(2,1)S(1)}, u32[]{:S(2)}, u32[]{:S(2)}) collective-permute-start(bf16[144,1792]{1,0:T(8,128)(2,1)S(1)} %get-tuple-element.68), channel_id=1, source_target_pairs={{0,12},{4,0},{8,4},{12,8},{1,13},{5,1},{9,5},{13,9},{2,14},{6,2},{... | collective-permute-start | bytes 1548296 | tf_op jit(solution)/shard_map/ppermute | solution.py:19
  497.5 22.2 %collective-permute-start.81 = (bf16[144,1792]{1,0:T(8,128)(2,1)S(1)}, bf16[144,1792]{1,0:T(8,128)(2,1)S(1)}, u32[]{:S(2)}, u32[]{:S(2)}) collective-permute-start(bf16[144,1792]{1,0:T(8,128)(2,1)S(1)} %get-tuple-element.69), channel_id=1, source_target_pairs={{0,4},{4,8},{8,12},{12,0},{1,5},{5,9},{9,13},{13,1},{2,6},{6,10},{... | collective-permute-start | bytes 1548296 | tf_op jit(solution)/shard_map/ppermute | solution.py:19
  500.0 21.5 %collective-permute-start.80 = (bf16[144,1792]{1,0:T(8,128)(2,1)S(1)}, bf16[144,1792]{1,0:T(8,128)(2,1)S(1)}, u32[]{:S(2)}, u32[]{:S(2)}) collective-permute-start(bf16[144,1792]{1,0:T(8,128)(2,1)S(1)} %get-tuple-element.66), channel_id=1, source_target_pairs={{0,8},{4,12},{8,0},{12,4},{1,9},{5,13},{9,1},{13,5},{2,10},{6,14},... | collective-permute-start | bytes 1548296 | tf_op jit(solution)/shard_map/ppermute | solution.py:19
  (153 other events, 1344.3 us)
